TPU v7x, 32 devices: a whole 2x2x4 slice. The times are simulated.
32 devices in a mesh: req: 8 (over z, y), tp: 4 (over x, core).
Axes of the slice: x: 2, y: 2, z: 4, core: 2. Of those that a mesh axis runs over, the one named last changes fastest.
Arguments:
- queries: bfloat16 [4096, 7168], P('req', 'tp')
- keys_new: bfloat16 [4096, 7168], P('req', 'tp')
- values_new: bfloat16 [4096, 7168], P('req', 'tp'), may hold values from -6 to 6
- cache_keys: bfloat16 [16, 1024, 7168], P('req', None, 'tp'), may hold values from -6 to 6
- cache_values: bfloat16 [16, 1024, 7168], P('req', None, 'tp'), may hold values from -6 to 6
- out_proj: bfloat16 [7168, 3584], P('tp'), may hold values from -0.0625 to 0.0625
- req_lengths: int32 [8, 4], P('req'), may hold values from 1 to 415, as said below
- cache_owner: int32 [8, 2], P('req'), may hold values from 0 to 7, as said below
- cache_slot: int32 [8, 2], P('req'), may hold values from 0 to 1
- prior_len: int32 [8, 2], P('req'), may hold values from 1 to 1024, as said below
Outputs:
- mixed: bfloat16 [4096, 3584], P(('req', 'tp'))
- new_keys: bfloat16 [16, 192, 7168], P('req', None, 'tp')
- new_values: bfloat16 [16, 192, 7168], P('req', None, 'tp')
Inputs may be any that keep to these rules, and one draw needn't show every extreme that they name: `req_lengths`: each row sums to 512; each continuing request has at most 192 new tokens, and some continuing request has exactly 192; continuing requests have at least 48 new tokens; some request has exactly 415. `cache_owner`: A continuing request's owner is the req index just before or just after its own, counted around the axis (index 0 follows index 7); the two continuing requests of one index have different owners; every cache slot of every index is used by exactly one continuing request. `prior_len`: some continuing request has exactly 1024 prior tokens.
All inputs are finite; a program needn't handle non-finite values.
Results may differ from a plain program's by a relative error of at most 0.014.
Values may be sent and summed in bfloat16 or wider, within the bound.
A program may use at most 128 MiB of HBM per device.

v0:
```python
import math

import jax
import jax.numpy as jnp
from jax import lax
from jax.sharding import PartitionSpec as P

HD = 224
NEWCAP = 192


shift_steps = (1, -1)
floor_value = -1e30


def shifted(value, axis, steps):
    count = lax.axis_size(axis)
    pairs = [(source, (source + steps) % count) for source in range(count)]
    return lax.ppermute(value, axis, pairs)


def attend_part(query_rows, key_rows, value_rows, live_mask, head_count):
    row_count = query_rows.shape[0]
    key_count = key_rows.shape[0]
    query_heads = query_rows.reshape(row_count, head_count, HD)
    key_heads = key_rows.reshape(key_count, head_count, HD)
    value_heads = value_rows.reshape(key_count, head_count, HD)
    scores = jnp.einsum(
        "thd,shd->hts", query_heads, key_heads, preferred_element_type=jnp.float32
    ) * (1.0 / math.sqrt(HD))
    scores = jnp.where(live_mask[None], scores, floor_value)
    row_top = jnp.max(scores, axis=2)
    weights = jnp.where(live_mask[None], jnp.exp(scores - row_top[:, :, None]), 0.0)
    row_total = jnp.sum(weights, axis=2)
    numerator = jnp.einsum(
        "hts,shd->thd",
        weights.astype(jnp.bfloat16),
        value_heads,
        preferred_element_type=jnp.float32,
    )
    return (numerator.reshape(row_count, head_count * HD), row_top.T, row_total.T)


def body(
    queries,
    keys_new,
    values_new,
    cache_keys,
    cache_values,
    out_proj,
    req_lengths,
    cache_owner,
    cache_slot,
    prior_len,
):
    tok_count = queries.shape[0]
    feat_width = queries.shape[1]
    head_count = feat_width // HD
    slot_count = cache_keys.shape[0]
    prior_rows = cache_keys.shape[1]
    req_lens = req_lengths[0]
    req_ends = jnp.cumsum(req_lens)
    starts = req_ends - req_lens
    positions = jnp.arange(tok_count, dtype=jnp.int32)
    segment = jnp.sum((positions[:, None] >= req_ends[None, :]).astype(jnp.int32), axis=1)
    own_live = (segment[:, None] == segment[None, :]) & (positions[None, :] <= positions[:, None])
    own_numer, own_top, own_total = attend_part(queries, keys_new, values_new, own_live, head_count)
    req_count = lax.axis_size("req")
    req_index = lax.axis_index("req")
    raw_offset = (cache_owner[0] - req_index + req_count) % req_count
    offset = jnp.where(raw_offset == req_count - 1, -1, raw_offset)
    row_marks = jnp.arange(NEWCAP, dtype=jnp.int32)
    slot_ids = jnp.arange(slot_count, dtype=jnp.int32)
    prior_marks = jnp.arange(prior_rows, dtype=jnp.int32)

    def rows_of(source, j):
        padded = jnp.pad(source, ((0, NEWCAP), (0, 0)))
        return lax.dynamic_slice_in_dim(padded, starts[j], NEWCAP, 0)

    valid_rows = [row_marks < req_lens[j] for j in range(slot_count)]
    query_rows = [rows_of(queries, j) for j in range(slot_count)]
    key_rows = [
        jnp.where(valid_rows[j][:, None], rows_of(keys_new, j), jnp.zeros((), jnp.bfloat16))
        for j in range(slot_count)
    ]
    value_rows = [
        jnp.where(valid_rows[j][:, None], rows_of(values_new, j), jnp.zeros((), jnp.bfloat16))
        for j in range(slot_count)
    ]
    tag_rows = [
        jnp.stack([cache_slot[0, j], jnp.int32(1), prior_len[0, j]]) for j in range(slot_count)
    ]

    def select_for(distance, items):
        chosen = jnp.zeros_like(items[0])
        for j in range(slot_count):
            chosen = jnp.where(offset[j] == distance, items[j], chosen)
        return chosen

    new_keys = jnp.zeros((slot_count, NEWCAP, feat_width), jnp.bfloat16)
    new_values = jnp.zeros((slot_count, NEWCAP, feat_width), jnp.bfloat16)
    chosen_keys = [jnp.zeros((prior_rows, feat_width), jnp.bfloat16) for j in range(slot_count)]
    chosen_values = [jnp.zeros((prior_rows, feat_width), jnp.bfloat16) for j in range(slot_count)]
    for distance in shift_steps:
        fetched_keys, fetched_values = shifted((cache_keys, cache_values), "req", -distance)
        for j in range(slot_count):
            is_owner = offset[j] == distance
            chosen_keys[j] = jnp.where(
                is_owner,
                lax.dynamic_index_in_dim(fetched_keys, cache_slot[0, j], 0, keepdims=False),
                chosen_keys[j],
            )
            chosen_values[j] = jnp.where(
                is_owner,
                lax.dynamic_index_in_dim(fetched_values, cache_slot[0, j], 0, keepdims=False),
                chosen_values[j],
            )
        got_keys, got_values, got_tag = shifted(
            (
                select_for(distance, key_rows),
                select_for(distance, value_rows),
                select_for(distance, tag_rows),
            ),
            "req",
            distance,
        )
        stored_keys = new_keys
        stored_values = new_values
        is_target = (slot_ids == got_tag[0]) & (got_tag[1] == 1)
        stored_keys = jnp.where(is_target[:, None, None], got_keys[None], stored_keys)
        stored_values = jnp.where(is_target[:, None, None], got_values[None], stored_values)
        new_keys = stored_keys
        new_values = stored_values
    results = []
    for j in range(slot_count):
        live_mask = jnp.broadcast_to(prior_marks[None, :] < prior_len[0, j], (NEWCAP, prior_rows))
        results.append(
            attend_part(query_rows[j], chosen_keys[j], chosen_values[j], live_mask, head_count)
        )
    full_numer = jnp.zeros((tok_count + NEWCAP, feat_width), jnp.float32)
    full_top = jnp.full((tok_count + NEWCAP, head_count), floor_value, jnp.float32)
    full_total = jnp.zeros((tok_count + NEWCAP, head_count), jnp.float32)
    for j in range(slot_count):
        keep = valid_rows[j][:, None]
        full_numer = lax.dynamic_update_slice_in_dim(
            full_numer, jnp.where(keep, results[j][0], 0.0), starts[j], 0
        )
        full_top = lax.dynamic_update_slice_in_dim(
            full_top, jnp.where(keep, results[j][1], floor_value), starts[j], 0
        )
        full_total = lax.dynamic_update_slice_in_dim(
            full_total, jnp.where(keep, results[j][2], 0.0), starts[j], 0
        )
    prior_numer = full_numer[:tok_count]
    prior_top = full_top[:tok_count]
    prior_total = full_total[:tok_count]
    both_top = jnp.maximum(own_top, prior_top)
    own_scale = jnp.exp(own_top - both_top)
    prior_scale = jnp.exp(prior_top - both_top)
    denominator = own_total * own_scale + prior_total * prior_scale
    numerator = (
        own_numer.reshape(tok_count, head_count, HD) * own_scale[:, :, None]
        + prior_numer.reshape(tok_count, head_count, HD) * prior_scale[:, :, None]
    )
    attended = (
        (numerator / denominator[:, :, None]).reshape(tok_count, feat_width).astype(jnp.bfloat16)
    )
    mixed = lax.psum_scatter(
        jnp.dot(attended, out_proj, preferred_element_type=jnp.float32).astype(jnp.bfloat16),
        "tp",
        scatter_dimension=0,
        tiled=True,
    )
    return (mixed, new_keys, new_values)


def solution(mesh):
    in_specs = (
        P("req", "tp"),
        P("req", "tp"),
        P("req", "tp"),
        P("req", None, "tp"),
        P("req", None, "tp"),
        P("tp", None),
        P("req", None),
        P("req", None),
        P("req", None),
        P("req", None),
    )
    out_specs = (P(("req", "tp"), None), P("req", None, "tp"), P("req", None, "tp"))
    return jax.shard_map(body, mesh=mesh, in_specs=in_specs, out_specs=out_specs, check_vma=False)
```

profile of v0, /device:TPU:0, one launch (start us, length us, event | category | flops | bytes accessed | tf_op | source)
XLA Modules:
  0.0 825.4 jit_solution(4674680329131561279)
XLA Ops:
  7.2 9.9 %copy.41 = bf16[2,1024,1792]{1,2,0:T(8,128)(2,1)} copy(bf16[2,1024,1792]{2,1,0:T(8,128)(2,1)} %param.13) | data formatting | bytes 14680064 | tf_op args[3]
  17.2 3.0 collective-permute-start
  20.2 3.1 collective-permute-start.1
  23.3 10.0 %copy.45 = bf16[2,1024,1792]{1,2,0:T(8,128)(2,1)} copy(bf16[2,1024,1792]{2,1,0:T(8,128)(2,1)} %param.14) | data formatting | bytes 14680064 | tf_op args[4]
  33.3 4.7 collective-permute-start.3
  38.0 0.6 fusion.73
  41.0 0.6 fusion.72
  44.4 0.6 fusion.71
  47.6 2.3 copy.37
  51.2 0.7 pad_dynamic-slice_fusion.4
  51.9 2.0 reshape.197
  53.9 1.1 reshape.198
  55.1 3.8 copy.38
  58.9 2.3 copy.39
  62.5 0.6 fusion.70
  63.1 0.6 iota_compare_fusion.3
  63.8 0.7 iota_compare_fusion.2
  64.4 0.6 fusion.69
  65.0 1.3 iota_compare_fusion.4
  66.6 3.9 fusion
  70.5 2.0 fusion.1
  72.6 1.2 copy-done
  73.7 419.8 %collective-permute-done = bf16[2,1024,1792]{1,2,0:T(8,128)(2,1)} collective-permute-done((bf16[2,1024,1792]{1,2,0:T(8,128)(2,1)}, bf16[2,1024,1792]{1,2,0:T(8,128)(2,1)}, u32[]{:S(2)}, u32[]{:S(2)}) %collective-permute-start) | collective-permute-done | bytes 7340064 | tf_op jit(solution)/shard_map/ppermute | solution.py:19
  493.5 2.5 collective-permute-done.1
  496.0 153.6 %collective-permute-done.2 = bf16[2,1024,1792]{1,2,0:T(8,128)(2,1)} collective-permute-done((bf16[2,1024,1792]{1,2,0:T(8,128)(2,1)}, bf16[2,1024,1792]{1,2,0:T(8,128)(2,1)}, u32[]{:S(2)}, u32[]{:S(2)}) %collective-permute-start.2) | collective-permute-done | bytes 7340064 | tf_op jit(solution)/shard_map/ppermute | solution.py:19
  649.6 2.2 collective-permute-done.3
  651.8 14.0 %select_select_fusion = (bf16[1,1024,1792]{1,2,0:T(8,128)(2,1)}, bf16[1,1024,1792]{1,2,0:T(8,128)(2,1)}, bf16[1,1024,1792]{1,2,0:T(8,128)(2,1)}, bf16[1,1024,1792]{1,2,0:T(8,128)(2,1)S(1)}) fusion(bf16[2,1024,1792]{1,2,0:T(8,128)(2,1)} %collective-permute-done.3, s32[]{:T(128)S(6)} %select_n.268, bf16[2,1024,1792]{1,2,0:T(8,128)(2,1)} %collective-permute-done.2, ...), kind=kLoop, calls=%fused_computation.26 | loop fusion | flops 14680064 | bytes 44040204 | tf_op jit(solution)/shard_map/jit(_where)/select_n | solution.py:113
  665.8 1.6 fusion.4
  667.4 1.9 fusion.7
  669.5 1.6 fusion.38
  671.1 0.9 copy.49
  672.0 1.8 reshape.200
  673.8 2.6 broadcast_select_fusion
  676.5 2.7 copy.50
  679.2 3.6 fusion.3
  682.8 1.7 fusion.5
  684.6 0.3 copy-done.4
  684.8 1.6 fusion.35
  686.5 0.9 copy.47
  687.4 1.8 reshape.199
  689.2 1.5 broadcast_select_fusion.1
  690.7 1.7 copy.48
  692.4 2.8 broadcast_in_dim.210
  695.2 9.8 %dynamic_update_slice.20 = f32[704,1792]{0,1:T(8,128)} dynamic-update-slice(f32[704,1792]{0,1:T(8,128)} %broadcast_in_dim.210, f32[192,1792]{0,1:T(8,128)} %copy.48, s32[]{:T(128)S(6)} %select_n.254, s32[]{:T(128)} %constant.64.clone.1) | dynamic-update-slice | bytes 2752516 | tf_op jit(solution)/shard_map/dynamic_update_slice | solution.py:145
  705.1 10.9 %dynamic_update_slice.21 = f32[704,1792]{0,1:T(8,128)} dynamic-update-slice(f32[704,1792]{0,1:T(8,128)} %dynamic_update_slice.20, f32[192,1792]{0,1:T(8,128)} %copy.50, s32[]{:T(128)S(6)} %select_n.266, s32[]{:T(128)} %constant.64.clone.1) | dynamic-update-slice | bytes 2752516 | tf_op jit(solution)/shard_map/dynamic_update_slice | solution.py:145
  716.0 4.2 slice.105
  720.2 0.2 dynamic_update_slice.18
  720.5 0.3 dynamic_update_slice.19
  720.8 0.3 dynamic_update_slice.22
  721.1 0.6 dynamic_update_slice.23
  721.7 7.9 fusion.18
  729.6 13.0 %convolution_convert_fusion = bf16[512,3584]{1,0:T(8,128)(2,1)} fusion(bf16[512,1792]{0,1:T(8,128)(2,1)S(1)} %bitcast.84, bf16[1792,3584]{1,0:T(8,128)(2,1)} %param.15), kind=kOutput, calls=%fused_computation.7 | convolution fusion | flops 6578503680 | bytes 18350080 | tf_op jit(solution)/shard_map/dot_general | solution.py:169
  742.6 5.0 select_select_fusion.7
  747.6 3.6 collective-permute-start.5
  751.1 4.7 collective-permute-start.8
  755.9 2.6 broadcast_select_fusion.5
  758.4 4.7 collective-permute-start.4
  763.1 2.6 broadcast_select_fusion.3
  765.7 42.2 %collective-permute-done.4 = s32[3]{0:T(128)S(1)} collective-permute-done((s32[3]{0:T(128)S(1)}, s32[3]{0:T(128)S(1)}, u32[]{:S(2)}, u32[]{:S(2)}) %collective-permute-start.4) | collective-permute-done | bytes 44 | tf_op jit(solution)/shard_map/ppermute | solution.py:19
  807.9 0.6 fusion.67
  809.1 5.0 collective-permute-done.6
  814.1 0.6 fusion.68
  815.4 1.3 compare_and_fusion
  816.7 1.9 select_select_fusion.4
  (43 shorter events, 0.7 us)
Async XLA Ops:
  7.2 811.4 %reduce-scatter.2.cloned.1.call-start = ((), (), s32[]{:S(2)}) async-start(), calls=%async_computation.1 | async-start | bytes 4587520 | tf_op jit(solution)/shard_map/reduce_scatter | solution.py:168
  17.2 20.8 %copy-start.8 = (s32[1,2]{1,0:T(1,128)S(1)}, s32[1,2]{1,0:T(1,128)}, u32[]{:S(2)}) copy-start(s32[1,2]{1,0:T(1,128)} %param.18) | copy-start | bytes 28
  17.2 23.8 %copy-start.11 = (s32[1,2]{1,0:T(1,128)S(1)}, s32[1,2]{1,0:T(1,128)}, u32[]{:S(2)}) copy-start(s32[1,2]{1,0:T(1,128)} %param.17) | copy-start | bytes 28
  17.2 27.0 %copy-start.10 = (s32[1,4]{1,0:T(1,128)S(1)}, s32[1,4]{1,0:T(1,128)}, u32[]{:S(2)}) copy-start(s32[1,4]{1,0:T(1,128)} %param.16) | copy-start | bytes 52
  17.2 30.4 %copy-start.1 = (bf16[512,1792]{1,0:T(8,128)(2,1)S(1)}, bf16[512,1792]{1,0:T(8,128)(2,1)}, u32[]{:S(2)}) copy-start(bf16[512,1792]{1,0:T(8,128)(2,1)} %param.10) | copy-start | bytes 5505028
  17.2 476.3 %collective-permute-start = (bf16[2,1024,1792]{1,2,0:T(8,128)(2,1)}, bf16[2,1024,1792]{1,2,0:T(8,128)(2,1)}, u32[]{:S(2)}, u32[]{:S(2)}) collective-permute-start(bf16[2,1024,1792]{1,2,0:T(8,128)(2,1)} %copy.41), channel_id=1, source_target_pairs={{0,4},{4,8},{8,12},{12,16},{16,20},{20,24},{24,28},{28,0},{1,5},{5... | collective-permute-start | bytes 22020104 | tf_op jit(solution)/shard_map/ppermute | solution.py:19
  20.2 475.8 %collective-permute-start.1 = (bf16[2,1024,1792]{1,2,0:T(8,128)(2,1)}, bf16[2,1024,1792]{1,2,0:T(8,128)(2,1)}, u32[]{:S(2)}, u32[]{:S(2)}) collective-permute-start(bf16[2,1024,1792]{1,2,0:T(8,128)(2,1)} %copy.41), channel_id=1, source_target_pairs={{0,28},{4,0},{8,4},{12,8},{16,12},{20,16},{24,20},{28,24},{1,29},{... | collective-permute-start | bytes 22020104 | tf_op jit(solution)/shard_map/ppermute | solution.py:19
  33.3 616.4 %collective-permute-start.2 = (bf16[2,1024,1792]{1,2,0:T(8,128)(2,1)}, bf16[2,1024,1792]{1,2,0:T(8,128)(2,1)}, u32[]{:S(2)}, u32[]{:S(2)}) collective-permute-start(bf16[2,1024,1792]{1,2,0:T(8,128)(2,1)} %copy.45), channel_id=1, source_target_pairs={{0,4},{4,8},{8,12},{12,16},{16,20},{20,24},{24,28},{28,0},{1,5},{5... | collective-permute-start | bytes 22020104 | tf_op jit(solution)/shard_map/ppermute | solution.py:19
  33.3 618.6 %collective-permute-start.3 = (bf16[2,1024,1792]{1,2,0:T(8,128)(2,1)}, bf16[2,1024,1792]{1,2,0:T(8,128)(2,1)}, u32[]{:S(2)}, u32[]{:S(2)}) collective-permute-start(bf16[2,1024,1792]{1,2,0:T(8,128)(2,1)} %copy.45), channel_id=1, source_target_pairs={{0,28},{4,0},{8,4},{12,8},{16,12},{20,16},{24,20},{28,24},{1,29},{... | collective-permute-start | bytes 22020104 | tf_op jit(solution)/shard_map/ppermute | solution.py:19
  51.9 7.1 copy-start.2
  55.1 7.4 copy-start.9
  66.6 3.9 copy-start.6
  70.5 3.2 copy-start
  667.4 2.0 copy-start.5
  673.8 5.3 copy-start.3
  682.8 2.0 copy-start.4
  716.0 5.7 copy-start.7
  747.6 69.1 %collective-permute-start.5 = (bf16[192,1792]{1,0:T(8,128)(2,1)S(1)}, bf16[192,1792]{1,0:T(8,128)(2,1)S(1)}, u32[]{:S(2)}, u32[]{:S(2)}) collective-permute-start(bf16[192,1792]{1,0:T(8,128)(2,1)S(1)} %get-tuple-element.19), channel_id=1, source_target_pairs={{0,28},{4,0},{8,4},{12,8},{16,12},{20,16},{24,20},{28,24},{1,29},{... | collective-permute-start | bytes 2064392 | tf_op jit(solution)/shard_map/ppermute | solution.py:19
  751.1 65.5 %collective-permute-start.7 = (bf16[192,1792]{1,0:T(8,128)(2,1)S(1)}, bf16[192,1792]{1,0:T(8,128)(2,1)S(1)}, u32[]{:S(2)}, u32[]{:S(2)}) collective-permute-start(bf16[192,1792]{1,0:T(8,128)(2,1)S(1)} %get-tuple-element.18), channel_id=1, source_target_pairs={{0,4},{4,8},{8,12},{12,16},{16,20},{20,24},{24,28},{28,0},{1,5},{5... | collective-permute-start | bytes 2064392 | tf_op jit(solution)/shard_map/ppermute | solution.py:19
  751.1 65.5 %collective-permute-start.8 = (bf16[192,1792]{1,0:T(8,128)(2,1)S(1)}, bf16[192,1792]{1,0:T(8,128)(2,1)S(1)}, u32[]{:S(2)}, u32[]{:S(2)}) collective-permute-start(bf16[192,1792]{1,0:T(8,128)(2,1)S(1)} %get-tuple-element.10), channel_id=1, source_target_pairs={{0,28},{4,0},{8,4},{12,8},{16,12},{20,16},{24,20},{28,24},{1,29},{... | collective-permute-start | bytes 2064392 | tf_op jit(solution)/shard_map/ppermute | solution.py:19
  755.8 60.8 %collective-permute-start.9 = (bf16[192,1792]{1,0:T(8,128)(2,1)S(1)}, bf16[192,1792]{1,0:T(8,128)(2,1)S(1)}, u32[]{:S(2)}, u32[]{:S(2)}) collective-permute-start(bf16[192,1792]{1,0:T(8,128)(2,1)S(1)} %get-tuple-element.11), channel_id=1, source_target_pairs={{0,4},{4,8},{8,12},{12,16},{16,20},{20,24},{24,28},{28,0},{1,5},{5... | collective-permute-start | bytes 2064392 | tf_op jit(solution)/shard_map/ppermute | solution.py:19
  758.4 49.5 %collective-permute-start.4 = (s32[3]{0:T(128)S(1)}, s32[3]{0:T(128)S(1)}, u32[]{:S(2)}, u32[]{:S(2)}) collective-permute-start(s32[3]{0:T(128)S(1)} %broadcast_select_fusion.5), channel_id=1, source_target_pairs={{0,28},{4,0},{8,4},{12,8},{16,12},{20,16},{24,20},{28,24},{1,29},{... | collective-permute-start | bytes 44 | tf_op jit(solution)/shard_map/ppermute | solution.py:19
  807.9 6.2 collective-permute-start.6
Sparse Core Ops, SparseCore 0:
  742.7 41.1 reduce-scatter.1
where the time goes:
time: 827 us; the launch traced here: 825 us
  waiting for transfers between devices  625 us (76%)
  local copies, waits for them, and re-layouts  77 us (9%)
  other arithmetic  40.2 us (5%)
  matrix products  33.2 us (4%)
  between operations  25.8 us (3%)
  starting transfers between devices  23.9 us (3%)
    ppermute x10, waiting for transfers between devices, shifted(): return lax.ppermute(value, axis, pairs)  625 us
    unnamed x29, local copies, waits for them, and re-layouts  30 us
    ppermute x10, starting transfers between devices, shifted(): return lax.ppermute(value, axis, pairs)  23.9 us
    dynamic_update_slice x2, local copies, waits for them, and re-layouts, body(): lax.dynamic_update_slice_in_dim(full_numer, jnp.where(keep, results[j][0]...  20.8 us
  transfers between devices with their start and end apart: 11, of which 6 were waited for; matrix products, arithmetic and copies ran while one was open for 6% of the time, Pallas kernels for 0%

commit v1 on v0

v1 whole, which is shorter than its diff:
```python
import math

import jax
import jax.numpy as jnp
from jax import lax
from jax.experimental import pallas as pl
from jax.experimental.pallas import tpu as pltpu
from jax.sharding import PartitionSpec as P

HD = 224
NEWCAP = 192
LANES = 128
GROUP = 4
WIDTH = GROUP * HD
FLOOR = -1e30
SCALE = 1.0 / math.sqrt(HD)
VMEM_LIMIT = 48 * 1024 * 1024


def shifted(value, axis, steps):
    count = lax.axis_size(axis)
    pairs = [(source, (source + steps) % count) for source in range(count)]
    return lax.ppermute(value, axis, pairs)


def lane_iota(rows, columns):
    return lax.broadcasted_iota(jnp.int32, (rows, columns), 1)


def attend_heads(query, key, value, live):
    rows = query.shape[0]
    tiles = [None] * (WIDTH // LANES)
    logs = []
    for head in range(GROUP):
        low, high = head * HD, (head + 1) * HD
        first, last = low // LANES, -(-high // LANES)
        a, b = first * LANES, last * LANES
        columns = lane_iota(rows, b - a)
        inside = (columns >= low - a) & (columns < high - a)
        part = jnp.where(inside, query[:, a:b], jnp.zeros((), query.dtype))
        scores = lax.dot_general(
            part, key[:, a:b], (((1,), (1,)), ((), ())), preferred_element_type=jnp.float32
        )
        scores = jnp.where(live, scores * SCALE, FLOOR)
        top = jnp.max(scores, axis=1, keepdims=True)
        weights = jnp.exp(scores - top)
        total = jnp.sum(weights, axis=1, keepdims=True)
        out = jnp.dot(
            weights.astype(jnp.bfloat16), value[:, a:b], preferred_element_type=jnp.float32
        ) / total
        logs.append(top + jnp.log(total))
        for tile in range(first, last):
            piece = out[:, tile * LANES - a : (tile + 1) * LANES - a]
            if tile * LANES < low:
                piece = jnp.where(
                    lane_iota(rows, LANES) >= low - tile * LANES, piece, tiles[tile]
                )
            tiles[tile] = piece
    return tiles, logs


def own_kernel(starts_ref, query_ref, key_ref, value_ref, out_ref, log_ref):
    group = pl.program_id(0)
    rows = query_ref.shape[0]
    block = 256

    @pl.when(group == 0)
    def _():
        log_ref[...] = jnp.zeros_like(log_ref)

    for begin in range(0, rows, block):
        end = begin + block
        row = begin + lax.broadcasted_iota(jnp.int32, (block, end), 0)
        column = lane_iota(block, end)
        first = jnp.zeros((block, end), jnp.int32)
        for j in range(1, starts_ref.shape[0]):
            first = jnp.where(row >= starts_ref[j], starts_ref[j], first)
        live = (column >= first) & (column <= row)
        tiles, logs = attend_heads(
            query_ref[begin:end, :], key_ref[:end, :], value_ref[:end, :], live
        )
        for tile, piece in enumerate(tiles):
            out_ref[begin:end, tile * LANES : (tile + 1) * LANES] = piece.astype(out_ref.dtype)
        lanes = lane_iota(block, LANES)
        stat = log_ref[begin:end, :]
        for head in range(GROUP):
            stat = jnp.where(lanes == group * GROUP + head, logs[head], stat)
        log_ref[begin:end, :] = stat


def prior_kernel(info_ref, query_ref, key_ref, value_ref, out_ref):
    group = pl.program_id(0)
    rows = query_ref.shape[0]
    feat = out_ref.shape[1] - LANES

    @pl.when(group == 0)
    def _():
        out_ref[:, feat:] = jnp.zeros((rows, LANES), out_ref.dtype)

    live = lane_iota(rows, key_ref.shape[1]) < info_ref[1]
    tiles, logs = attend_heads(query_ref[...], key_ref[0], value_ref[0], live)
    for tile, piece in enumerate(tiles):
        place = pl.ds(pl.multiple_of(group * WIDTH + tile * LANES, LANES), LANES)
        out_ref[:, place] = piece.astype(out_ref.dtype)
    lanes = lane_iota(rows, LANES)
    stat = out_ref[:, feat:].astype(jnp.float32)
    for head in range(GROUP):
        rest = logs[head]
        for part in range(3):
            rounded = rest.astype(jnp.bfloat16).astype(jnp.float32)
            stat = jnp.where(lanes == (group * GROUP + head) * 3 + part, rounded, stat)
            rest = rest - rounded
    out_ref[:, feat:] = stat.astype(out_ref.dtype)


def project_kernel(info_ref, own_ref, log_ref, plus_ref, minus_ref, weight_ref, out_ref, held):
    rows, feat = own_ref.shape
    cap = plus_ref.shape[0]

    @pl.when(pl.program_id(0) == 0)
    def _():
        spread = []
        row = lax.broadcasted_iota(jnp.int32, (rows, cap), 0)
        column = lane_iota(rows, cap)
        for d in range(2):
            start, count = info_ref[2 * d], info_ref[2 * d + 1]
            hit = (row - start == column) & (column < count)
            spread.append(jnp.where(hit, 1.0, 0.0).astype(jnp.bfloat16))

        def placed(a, b):
            return jnp.dot(
                spread[0], plus_ref[:, a:b], preferred_element_type=jnp.float32
            ) + jnp.dot(spread[1], minus_ref[:, a:b], preferred_element_type=jnp.float32)

        stat = placed(feat, feat + LANES)
        mine = log_ref[...]
        marks = lax.broadcasted_iota(jnp.int32, (rows, 1), 0)
        has = marks < info_ref[1] + info_ref[3]
        own_part, prior_part = [], []
        for head in range(feat // HD):
            far = stat[:, 3 * head : 3 * head + 1]
            far = far + stat[:, 3 * head + 1 : 3 * head + 2]
            far = far + stat[:, 3 * head + 2 : 3 * head + 3]
            near = mine[:, head : head + 1]
            top = jnp.maximum(near, far)
            x, y = jnp.exp(near - top), jnp.exp(far - top)
            own_part.append(jnp.where(has, x / (x + y), 1.0))
            prior_part.append(jnp.where(has, y / (x + y), 0.0))
        lanes = lane_iota(rows, LANES)
        for tile in range(feat // LANES):
            a, b = tile * LANES, (tile + 1) * LANES
            h0, h1 = a // HD, (b - 1) // HD
            x, y = own_part[h0], prior_part[h0]
            if h1 != h0:
                x = jnp.where(lanes < h1 * HD - a, x, own_part[h1])
                y = jnp.where(lanes < h1 * HD - a, y, prior_part[h1])
            both = own_ref[:, a:b].astype(jnp.float32) * x + placed(a, b) * y
            held[:, a:b] = both.astype(jnp.bfloat16)

    out_ref[...] = jnp.dot(
        held[...], weight_ref[...], preferred_element_type=jnp.float32
    ).astype(out_ref.dtype)


def own_attention(starts, queries, keys, values):
    rows, feat = queries.shape
    spec = pl.BlockSpec((rows, WIDTH), lambda g, s: (0, g))
    return pl.pallas_call(
        own_kernel,
        grid_spec=pltpu.PrefetchScalarGridSpec(
            num_scalar_prefetch=1,
            grid=(feat // WIDTH,),
            in_specs=[spec] * 3,
            out_specs=[spec, pl.BlockSpec((rows, LANES), lambda g, s: (0, 0))],
        ),
        out_shape=[
            jax.ShapeDtypeStruct((rows, feat), jnp.bfloat16),
            jax.ShapeDtypeStruct((rows, LANES), jnp.float32),
        ],
        compiler_params=pltpu.CompilerParams(vmem_limit_bytes=VMEM_LIMIT),
        cost_estimate=pl.CostEstimate(
            flops=20_000_000_000, bytes_accessed=9_000_000, transcendentals=2_000_000
        ),
        name="own_attention",
    )(starts, queries, keys, values)


def prior_attention(info, queries, cache_keys, cache_values):
    rows, feat = queries.shape
    prior = cache_keys.shape[1]
    cache = pl.BlockSpec((1, prior, WIDTH), lambda g, s: (s[0], 0, g))
    return pl.pallas_call(
        prior_kernel,
        grid_spec=pltpu.PrefetchScalarGridSpec(
            num_scalar_prefetch=1,
            grid=(feat // WIDTH,),
            in_specs=[pl.BlockSpec((rows, WIDTH), lambda g, s: (0, g)), cache, cache],
            out_specs=pl.BlockSpec((rows, feat + LANES), lambda g, s: (0, 0)),
        ),
        out_shape=jax.ShapeDtypeStruct((rows, feat + LANES), jnp.bfloat16),
        compiler_params=pltpu.CompilerParams(vmem_limit_bytes=VMEM_LIMIT),
        cost_estimate=pl.CostEstimate(
            flops=10_000_000_000, bytes_accessed=9_000_000, transcendentals=2_000_000
        ),
        name="prior_attention",
    )(info, queries, cache_keys, cache_values)


def project(info, own, logs, plus, minus, weight):
    rows, feat = own.shape
    columns = weight.shape[1]
    block = 512

    def whole(array):
        return pl.BlockSpec(array.shape, lambda n, s: (0, 0))

    return pl.pallas_call(
        project_kernel,
        grid_spec=pltpu.PrefetchScalarGridSpec(
            num_scalar_prefetch=1,
            grid=(columns // block,),
            in_specs=[
                whole(own),
                whole(logs),
                whole(plus),
                whole(minus),
                pl.BlockSpec((feat, block), lambda n, s: (0, n)),
            ],
            out_specs=pl.BlockSpec((rows, block), lambda n, s: (0, n)),
            scratch_shapes=[pltpu.VMEM((rows, feat), jnp.bfloat16)],
        ),
        out_shape=jax.ShapeDtypeStruct((rows, columns), jnp.bfloat16),
        compiler_params=pltpu.CompilerParams(vmem_limit_bytes=VMEM_LIMIT),
        cost_estimate=pl.CostEstimate(
            flops=2 * rows * feat * columns, bytes_accessed=22_000_000, transcendentals=0
        ),
        name="project",
    )(info, own, logs, plus, minus, weight)


def pick_rows(source, start, count):
    row = lax.broadcasted_iota(jnp.int32, (NEWCAP, source.shape[0]), 0)
    column = lane_iota(NEWCAP, source.shape[0])
    hit = (column - start == row) & (row < count)
    return jnp.dot(
        hit.astype(jnp.bfloat16), source, preferred_element_type=jnp.float32
    ).astype(jnp.bfloat16)


def body(
    queries,
    keys_new,
    values_new,
    cache_keys,
    cache_values,
    out_proj,
    req_lengths,
    cache_owner,
    cache_slot,
    prior_len,
):
    slot_count = cache_keys.shape[0]
    lens = [req_lengths[0, j] for j in range(req_lengths.shape[1])]
    starts = [jnp.int32(0)]
    for j in range(1, len(lens)):
        starts.append(starts[-1] + lens[j - 1])
    count = lax.axis_size("req")
    me = lax.axis_index("req")
    next_is_first = cache_owner[0, 0] == lax.rem(me + 1, count)

    def by_way(a, b):
        return jnp.where(next_is_first, a, b), jnp.where(next_is_first, b, a)

    start = by_way(starts[0], starts[1])
    length = by_way(lens[0], lens[1])
    slot = by_way(cache_slot[0, 0], cache_slot[0, 1])
    prior = by_way(prior_len[0, 0], prior_len[0, 1])
    ways = (1, -1)

    tags = [shifted(jnp.stack([slot[d], prior[d]]), "req", ways[d]) for d in range(2)]
    asked = [shifted(pick_rows(queries, start[d], length[d]), "req", ways[d]) for d in range(2)]
    own, logs = own_attention(jnp.stack(starts), queries, keys_new, values_new)
    sent_keys = [pick_rows(keys_new, start[d], length[d]) for d in range(2)]
    sent_values = [pick_rows(values_new, start[d], length[d]) for d in range(2)]

    sent_keys, asked = lax.optimization_barrier((sent_keys, asked))
    got_keys = [shifted(sent_keys[d], "req", ways[d]) for d in range(2)]
    answers = [prior_attention(tags[d], asked[d], cache_keys, cache_values) for d in range(2)]
    back = [shifted(answers[d], "req", -ways[d]) for d in range(2)]
    sent_values, back = lax.optimization_barrier((sent_values, back))
    got_values = [shifted(sent_values[d], "req", ways[d]) for d in range(2)]

    info = jnp.stack([start[0], length[0], start[1], length[1]])
    mixed = project(info, own, logs, back[0], back[1], out_proj)
    mixed = lax.psum_scatter(mixed, "tp", scatter_dimension=0, tiled=True)

    slot_ids = jnp.arange(slot_count, dtype=jnp.int32)[:, None, None]
    new_keys = jnp.where(slot_ids == tags[0][0], got_keys[0][None], got_keys[1][None])
    new_values = jnp.where(slot_ids == tags[0][0], got_values[0][None], got_values[1][None])
    return (mixed, new_keys, new_values)


def solution(mesh):
    in_specs = (
        P("req", "tp"),
        P("req", "tp"),
        P("req", "tp"),
        P("req", None, "tp"),
        P("req", None, "tp"),
        P("tp", None),
        P("req", None),
        P("req", None),
        P("req", None),
        P("req", None),
    )
    out_specs = (P(("req", "tp"), None), P("req", None, "tp"), P("req", None, "tp"))
    return jax.shard_map(body, mesh=mesh, in_specs=in_specs, out_specs=out_specs, check_vma=False)
```

time: 827 us -> 196 us (0.24)
  waiting for transfers between devices: 625 us -> 86.1 us
  local copies, waits for them, and re-layouts: 77 us -> 5.42 us
  Pallas kernels: 0 us -> 40.7 us
  other arithmetic: 40.2 us -> 2.97 us
  matrix products: 33.2 us -> 9.83 us
    ppermute x10, waiting for transfers between devices: 625 us -> 86.1 us  [shifted(): return lax.ppermute(value, axis, pairs)]
    pallas_call x0 -> x4, Pallas kernels: none -> 40.7 us  [the longest x1 16.4 us: project(): pl.pallas_call(project_kernel, grid_spec=pltpu.PrefetchScalarGridSpec(num...]
    unnamed x29 -> x10, local copies, waits for them, and re-layouts: 30 us -> 1.3 us
    select_n x10 -> x1, other arithmetic: 30.1 us -> 1.85 us  [body(): jnp.where(slot_ids == tags[0][0], got_values[0][None], got_values[1][None])]
    dot_general x7 -> x6, matrix products: 33.2 us -> 9.83 us  [pick_rows(): jnp.dot(hit.astype(jnp.bfloat16), source, preferred_element_type=jnp.floa...]
    dynamic_update_slice x6 -> x0, local copies, waits for them, and re-layouts: 22.1 us -> none  [the longest x2 20.8 us: body(): lax.dynamic_update_slice_in_dim(full_numer, jnp.where(keep, results[j][0]...]
  transfers between devices with their start and end apart: 11 -> 11, of which waited for: 6 -> 8; matrix products, arithmetic and copies ran while one was open for 6% -> 7% of each run, Pallas kernels for 0% -> 12%
where the time goes in v1:
time: 196 us
  waiting for transfers between devices  86.1 us (44%)
  Pallas kernels  40.7 us (21%)
  between operations  25.7 us (13%)
  starting transfers between devices  25 us (13%)
  matrix products  9.83 us (5%)
  local copies, waits for them, and re-layouts  5.42 us (3%)
  other arithmetic  2.97 us (2%)
    ppermute x10, waiting for transfers between devices, shifted(): return lax.ppermute(value, axis, pairs)  86.1 us
    ppermute x10, starting transfers between devices, shifted(): return lax.ppermute(value, axis, pairs)  25 us
    pallas_call x1, Pallas kernels, project(): pl.pallas_call(project_kernel, grid_spec=pltpu.PrefetchScalarGridSpec(num...  16.4 us
    pallas_call x2, Pallas kernels, prior_attention(): pl.pallas_call(prior_kernel, grid_spec=pltpu.PrefetchScalarGridSpec(num_s...  16.3 us
    dot_general x6, matrix products, pick_rows(): jnp.dot(hit.astype(jnp.bfloat16), source, preferred_element_type=jnp.floa...  9.83 us
    pallas_call x1, Pallas kernels, own_attention(): pl.pallas_call(own_kernel, grid_spec=pltpu.PrefetchScalarGridSpec(num_sca...  7.96 us
  transfers between devices with their start and end apart: 11, of which 8 were waited for; matrix products, arithmetic and copies ran while one was open for 7% of the time, Pallas kernels for 12%

profile of v1, /device:TPU:0, one launch (start us, length us, event | category | flops | bytes accessed | tf_op | source)
XLA Modules:
  0.0 195.8 jit_solution(6341529223021547604)
XLA Ops:
  7.2 0.0 copy-start
  7.2 0.0 reduce-scatter.2.cloned.1.call-start
  7.2 1.4 fusion.20
  8.6 1.3 fusion.21
  13.1 0.1 pad_add_fusion.3
  13.1 6.0 %collective-permute-start.4 = (s32[2]{0:T(128)S(1)}, s32[2]{0:T(128)S(1)}, u32[]{:S(2)}, u32[]{:S(2)}) collective-permute-start(s32[2]{0:T(128)S(1)} %pad_add_fusion.3), channel_id=1, source_target_pairs={{0,28},{4,0},{8,4},{12,8},{16,12},{20,16},{24,20},{28,24},{1,29},{... | collective-permute-start | bytes 32 | tf_op jit(solution)/shard_map/ppermute | solution.py:23
  21.7 0.1 pad_add_fusion.2
  21.7 0.0 collective-permute-start
  21.7 1.4 fusion.22
  25.1 2.9 %convolution_convert_fusion.1 = bf16[192,1792]{1,0:T(8,128)(2,1)} fusion(bf16[512,1792]{1,0:T(8,128)(2,1)} %query_ref.1, s32[512]{0:T(512)S(1)} %iota_subtract_fusion.1, pred[192]{0:T(512)(128)(4,1)S(1)} %iota_compare_fusion.3), kind=kOutput, calls=%fused_computation.1 | convolution fusion | flops 352862208 | bytes 2525376 | tf_op jit(solution)/shard_map/dot_general | solution.py:245
  28.1 0.0 collective-permute-start.1
  30.0 0.0 copy-done
  30.0 1.4 convolution_convert_fusion
  31.5 4.7 %collective-permute-start.2 = (bf16[192,1792]{1,0:T(8,128)(2,1)}, bf16[192,1792]{1,0:T(8,128)(2,1)S(1)}, u32[]{:S(2)}, u32[]{:S(2)}) collective-permute-start(bf16[192,1792]{1,0:T(8,128)(2,1)} %convolution_convert_fusion), channel_id=1, source_target_pairs={{0,28},{4,0},{8,4},{12,8},{16,12},{20,16},{24,20},{28,24},{1,29},{... | collective-permute-start | bytes 2064392 | tf_op jit(solution)/shard_map/ppermute | solution.py:23
  38.2 0.0 copy-start.1
  38.2 0.8 pad_add_fusion.1.starts_ref
  39.0 2.9 %convolution_convert_fusion.2 = bf16[192,1792]{1,0:T(8,128)(2,1)} fusion(bf16[512,1792]{1,0:T(8,128)(2,1)} %key_ref.3, s32[512]{0:T(512)S(1)} %iota_subtract_fusion, pred[192]{0:T(512)(128)(4,1)S(1)} %iota_compare_fusion.2), kind=kOutput, calls=%fused_computation.2 | convolution fusion | flops 352862208 | bytes 2525376 | tf_op jit(solution)/shard_map/dot_general | solution.py:245
  41.9 0.0 copy-done.1
  41.9 1.4 convolution_convert_fusion.3
  43.3 14.5 %collective-permute-done.1.query_ref = bf16[192,1792]{1,0:T(8,128)(2,1)S(1)} collective-permute-done((bf16[192,1792]{1,0:T(8,128)(2,1)}, bf16[192,1792]{1,0:T(8,128)(2,1)S(1)}, u32[]{:S(2)}, u32[]{:S(2)}) %collective-permute-start.1) | collective-permute-done | bytes 688160 | tf_op jit(solution)/shard_map/ppermute | solution.py:23
  57.8 4.8 %collective-permute-done.2.query_ref = bf16[192,1792]{1,0:T(8,128)(2,1)S(1)} collective-permute-done((bf16[192,1792]{1,0:T(8,128)(2,1)}, bf16[192,1792]{1,0:T(8,128)(2,1)S(1)}, u32[]{:S(2)}, u32[]{:S(2)}) %collective-permute-start.2) | collective-permute-done | bytes 688160 | tf_op jit(solution)/shard_map/ppermute | solution.py:23
  62.6 0.0 collective-permute-done.4.info_ref
  62.6 8.2 %prior_attention.3 = bf16[192,1920]{1,0:T(8,128)(2,1)S(1)} custom-call(s32[2]{0:T(128)S(1)} %collective-permute-done.4.info_ref, bf16[192,1792]{1,0:T(8,128)(2,1)S(1)} %collective-permute-done.2.query_ref, bf16[2,1024,1792]{2,1,0:T(8,128)(2,1)} %key_ref.5, bf16[2,1024,1792]{2,1,0:T(8,128)(2,1)} %value_ref.5), custom_call_target="tpu_custom_call" | custom-call | flops 10000000000 | bytes 9000000 | tf_op jit(solution)/shard_map/prior_attention/pallas_call | solution.py:192
  70.8 0.1 collective-permute-start.5
  70.9 0.0 collective-permute-done.info_ref
  70.9 8.2 %prior_attention.2 = bf16[192,1920]{1,0:T(8,128)(2,1)S(1)} custom-call(s32[2]{0:T(128)S(1)} %collective-permute-done.info_ref, bf16[192,1792]{1,0:T(8,128)(2,1)S(1)} %collective-permute-done.1.query_ref, bf16[2,1024,1792]{2,1,0:T(8,128)(2,1)} %key_ref.5, bf16[2,1024,1792]{2,1,0:T(8,128)(2,1)} %value_ref.5), custom_call_target="tpu_custom_call" | custom-call | flops 10000000000 | bytes 9000000 | tf_op jit(solution)/shard_map/prior_attention/pallas_call | solution.py:192
  79.0 0.0 copy-start.2
  79.1 4.9 %collective-permute-start.3 = (bf16[192,1920]{1,0:T(8,128)(2,1)S(1)}, bf16[192,1920]{1,0:T(8,128)(2,1)S(1)}, u32[]{:S(2)}, u32[]{:S(2)}) collective-permute-start(bf16[192,1920]{1,0:T(8,128)(2,1)S(1)} %prior_attention.2), channel_id=1, source_target_pairs={{0,28},{4,0},{8,4},{12,8},{16,12},{20,16},{24,20},{28,24},{1,29},{... | collective-permute-start | bytes 2211848 | tf_op jit(solution)/shard_map/ppermute | solution.py:23
  84.0 8.0 %own_attention.1 = (bf16[512,1792]{1,0:T(8,128)(2,1)S(1)}, f32[512,128]{1,0:T(8,128)S(1)}) custom-call(s32[4]{0:T(128)S(1)} %pad_add_fusion.1.starts_ref, bf16[512,1792]{1,0:T(8,128)(2,1)S(1)} %copy-done, bf16[512,1792]{1,0:T(8,128)(2,1)S(1)} %copy-done.1, bf16[512,1792]{1,0:T(8,128)(2,1)} %value_ref.3), custom_call_target="tpu_custom_call" | custom-call | flops 20000000000 | bytes 9000000 | tf_op jit(solution)/shard_map/own_attention/pallas_call | solution.py:168
  92.0 0.1 pad_add_fusion.info_ref
  92.0 0.0 copy-done.2
  92.0 0.6 convolution_convert_fusion.4
  92.6 0.6 convolution_convert_fusion.5
  93.2 9.7 %collective-permute-done.5.minus_ref = bf16[192,1920]{1,0:T(8,128)(2,1)S(1)} collective-permute-done((bf16[192,1920]{1,0:T(8,128)(2,1)S(1)}, bf16[192,1920]{1,0:T(8,128)(2,1)S(1)}, u32[]{:S(2)}, u32[]{:S(2)}) %collective-permute-start.5) | collective-permute-done | bytes 737312 | tf_op jit(solution)/shard_map/ppermute | solution.py:23
  102.9 4.9 %collective-permute-done.3.plus_ref = bf16[192,1920]{1,0:T(8,128)(2,1)S(1)} collective-permute-done((bf16[192,1920]{1,0:T(8,128)(2,1)S(1)}, bf16[192,1920]{1,0:T(8,128)(2,1)S(1)}, u32[]{:S(2)}, u32[]{:S(2)}) %collective-permute-start.3) | collective-permute-done | bytes 737312 | tf_op jit(solution)/shard_map/ppermute | solution.py:23
  107.7 16.4 %project.1 = bf16[512,3584]{1,0:T(8,128)(2,1)} custom-call(s32[4]{0:T(128)S(1)} %pad_add_fusion.info_ref, bf16[512,1792]{1,0:T(8,128)(2,1)S(1)} %get-tuple-element.13.own_ref, f32[512,128]{1,0:T(8,128)S(1)} %get-tuple-element.14.log_ref, bf16[192,1920]{1,0:T(8,128)(2,1)S(1)} %collective-permute-done.3.plus_ref, ...), custom_call_target="tpu_custom_call" | custom-call | flops 6576668672 | bytes 22000000 | tf_op jit(solution)/shard_map/project/pallas_call | solution.py:217
  124.2 0.0 copy-start.4
  124.2 0.0 copy-start.3
  124.2 0.0 reduce-scatter.2.cloned.1.call-update
  124.2 1.1 copy-done.4
  125.3 0.0 collective-permute-start.6
  125.3 0.2 copy-done.3
  125.5 4.5 %collective-permute-start.7 = (bf16[192,1792]{1,0:T(8,128)(2,1)S(1)}, bf16[192,1792]{1,0:T(8,128)(2,1)S(1)}, u32[]{:S(2)}, u32[]{:S(2)}) collective-permute-start(bf16[192,1792]{1,0:T(8,128)(2,1)S(1)} %copy-done.3), channel_id=1, source_target_pairs={{0,28},{4,0},{8,4},{12,8},{16,12},{20,16},{24,20},{28,24},{1,29},{... | collective-permute-start | bytes 2064392 | tf_op jit(solution)/shard_map/ppermute | solution.py:23
  130.0 0.0 collective-permute-start.8
  130.0 4.7 %collective-permute-start.9 = (bf16[192,1792]{1,0:T(8,128)(2,1)S(1)}, bf16[192,1792]{1,0:T(8,128)(2,1)S(1)}, u32[]{:S(2)}, u32[]{:S(2)}) collective-permute-start(bf16[192,1792]{1,0:T(8,128)(2,1)S(1)} %convolution_convert_fusion.4), channel_id=1, source_target_pairs={{0,28},{4,0},{8,4},{12,8},{16,12},{20,16},{24,20},{28,24},{1,29},{... | collective-permute-start | bytes 2064392 | tf_op jit(solution)/shard_map/ppermute | solution.py:23
  134.7 35.6 %collective-permute-done.6 = bf16[192,1792]{1,0:T(8,128)(2,1)S(1)} collective-permute-done((bf16[192,1792]{1,0:T(8,128)(2,1)S(1)}, bf16[192,1792]{1,0:T(8,128)(2,1)S(1)}, u32[]{:S(2)}, u32[]{:S(2)}) %collective-permute-start.6) | collective-permute-done | bytes 688160 | tf_op jit(solution)/shard_map/ppermute | solution.py:23
  170.3 2.9 %collective-permute-done.7 = bf16[192,1792]{1,0:T(8,128)(2,1)S(1)} collective-permute-done((bf16[192,1792]{1,0:T(8,128)(2,1)S(1)}, bf16[192,1792]{1,0:T(8,128)(2,1)S(1)}, u32[]{:S(2)}, u32[]{:S(2)}) %collective-permute-start.7) | collective-permute-done | bytes 688160 | tf_op jit(solution)/shard_map/ppermute | solution.py:23
  173.2 11.4 %collective-permute-done.8 = bf16[192,1792]{1,0:T(8,128)(2,1)S(1)} collective-permute-done((bf16[192,1792]{1,0:T(8,128)(2,1)S(1)}, bf16[192,1792]{1,0:T(8,128)(2,1)S(1)}, u32[]{:S(2)}, u32[]{:S(2)}) %collective-permute-start.8) | collective-permute-done | bytes 688160 | tf_op jit(solution)/shard_map/ppermute | solution.py:23
  184.7 2.4 %collective-permute-done.9 = bf16[192,1792]{1,0:T(8,128)(2,1)S(1)} collective-permute-done((bf16[192,1792]{1,0:T(8,128)(2,1)S(1)}, bf16[192,1792]{1,0:T(8,128)(2,1)S(1)}, u32[]{:S(2)}, u32[]{:S(2)}) %collective-permute-start.9) | collective-permute-done | bytes 688160 | tf_op jit(solution)/shard_map/ppermute | solution.py:23
  187.1 1.9 broadcast_select_fusion
  188.9 0.0 reduce-scatter.2.cloned.1.call-done
  (5 shorter events, 0.1 us)
Async XLA Ops:
  7.2 22.9 %copy-start = (bf16[512,1792]{1,0:T(8,128)(2,1)S(1)}, bf16[512,1792]{1,0:T(8,128)(2,1)}, u32[]{:S(2)}) copy-start(bf16[512,1792]{1,0:T(8,128)(2,1)} %query_ref.1) | copy-start | bytes 5505028
  7.2 181.7 %reduce-scatter.2.cloned.1.call-start = ((), (), s32[]{:S(2)}) async-start(), calls=%async_computation.1 | async-start | bytes 4587520 | tf_op jit(solution)/shard_map/reduce_scatter | solution.py:295
  13.1 49.5 %collective-permute-start.4 = (s32[2]{0:T(128)S(1)}, s32[2]{0:T(128)S(1)}, u32[]{:S(2)}, u32[]{:S(2)}) collective-permute-start(s32[2]{0:T(128)S(1)} %pad_add_fusion.3), channel_id=1, source_target_pairs={{0,28},{4,0},{8,4},{12,8},{16,12},{20,16},{24,20},{28,24},{1,29},{... | collective-permute-start | bytes 32 | tf_op jit(solution)/shard_map/ppermute | solution.py:23
  21.7 49.1 %collective-permute-start = (s32[2]{0:T(128)S(1)}, s32[2]{0:T(128)S(1)}, u32[]{:S(2)}, u32[]{:S(2)}) collective-permute-start(s32[2]{0:T(128)S(1)} %pad_add_fusion.2), channel_id=1, source_target_pairs={{0,4},{4,8},{8,12},{12,16},{16,20},{20,24},{24,28},{28,0},{1,5},{5... | collective-permute-start | bytes 32 | tf_op jit(solution)/shard_map/ppermute | solution.py:23
  28.1 29.8 %collective-permute-start.1 = (bf16[192,1792]{1,0:T(8,128)(2,1)}, bf16[192,1792]{1,0:T(8,128)(2,1)S(1)}, u32[]{:S(2)}, u32[]{:S(2)}) collective-permute-start(bf16[192,1792]{1,0:T(8,128)(2,1)} %convolution_convert_fusion.1), channel_id=1, source_target_pairs={{0,4},{4,8},{8,12},{12,16},{16,20},{20,24},{24,28},{28,0},{1,5},{5... | collective-permute-start | bytes 2064392 | tf_op jit(solution)/shard_map/ppermute | solution.py:23
  31.5 31.1 %collective-permute-start.2 = (bf16[192,1792]{1,0:T(8,128)(2,1)}, bf16[192,1792]{1,0:T(8,128)(2,1)S(1)}, u32[]{:S(2)}, u32[]{:S(2)}) collective-permute-start(bf16[192,1792]{1,0:T(8,128)(2,1)} %convolution_convert_fusion), channel_id=1, source_target_pairs={{0,28},{4,0},{8,4},{12,8},{16,12},{20,16},{24,20},{28,24},{1,29},{... | collective-permute-start | bytes 2064392 | tf_op jit(solution)/shard_map/ppermute | solution.py:23
  38.2 3.8 %copy-start.1 = (bf16[512,1792]{1,0:T(8,128)(2,1)S(1)}, bf16[512,1792]{1,0:T(8,128)(2,1)}, u32[]{:S(2)}) copy-start(bf16[512,1792]{1,0:T(8,128)(2,1)} %key_ref.3) | copy-start | bytes 5505028
  70.8 32.1 %collective-permute-start.5 = (bf16[192,1920]{1,0:T(8,128)(2,1)S(1)}, bf16[192,1920]{1,0:T(8,128)(2,1)S(1)}, u32[]{:S(2)}, u32[]{:S(2)}) collective-permute-start(bf16[192,1920]{1,0:T(8,128)(2,1)S(1)} %prior_attention.3), channel_id=1, source_target_pairs={{0,4},{4,8},{8,12},{12,16},{16,20},{20,24},{24,28},{28,0},{1,5},{5... | collective-permute-start | bytes 2211848 | tf_op jit(solution)/shard_map/ppermute | solution.py:23
  79.0 13.0 %copy-start.2 = (bf16[512,1792]{1,0:T(8,128)(2,1)S(1)}, bf16[512,1792]{1,0:T(8,128)(2,1)}, u32[]{:S(2)}) copy-start(bf16[512,1792]{1,0:T(8,128)(2,1)} %value_ref.3) | copy-start | bytes 5505028
  79.1 28.7 %collective-permute-start.3 = (bf16[192,1920]{1,0:T(8,128)(2,1)S(1)}, bf16[192,1920]{1,0:T(8,128)(2,1)S(1)}, u32[]{:S(2)}, u32[]{:S(2)}) collective-permute-start(bf16[192,1920]{1,0:T(8,128)(2,1)S(1)} %prior_attention.2), channel_id=1, source_target_pairs={{0,28},{4,0},{8,4},{12,8},{16,12},{20,16},{24,20},{28,24},{1,29},{... | collective-permute-start | bytes 2211848 | tf_op jit(solution)/shard_map/ppermute | solution.py:23
  124.2 1.1 copy-start.4
  124.2 1.3 copy-start.3
  125.3 45.1 %collective-permute-start.6 = (bf16[192,1792]{1,0:T(8,128)(2,1)S(1)}, bf16[192,1792]{1,0:T(8,128)(2,1)S(1)}, u32[]{:S(2)}, u32[]{:S(2)}) collective-permute-start(bf16[192,1792]{1,0:T(8,128)(2,1)S(1)} %copy-done.4), channel_id=1, source_target_pairs={{0,4},{4,8},{8,12},{12,16},{16,20},{20,24},{24,28},{28,0},{1,5},{5... | collective-permute-start | bytes 2064392 | tf_op jit(solution)/shard_map/ppermute | solution.py:23
  125.5 47.8 %collective-permute-start.7 = (bf16[192,1792]{1,0:T(8,128)(2,1)S(1)}, bf16[192,1792]{1,0:T(8,128)(2,1)S(1)}, u32[]{:S(2)}, u32[]{:S(2)}) collective-permute-start(bf16[192,1792]{1,0:T(8,128)(2,1)S(1)} %copy-done.3), channel_id=1, source_target_pairs={{0,28},{4,0},{8,4},{12,8},{16,12},{20,16},{24,20},{28,24},{1,29},{... | collective-permute-start | bytes 2064392 | tf_op jit(solution)/shard_map/ppermute | solution.py:23
  130.0 54.7 %collective-permute-start.8 = (bf16[192,1792]{1,0:T(8,128)(2,1)S(1)}, bf16[192,1792]{1,0:T(8,128)(2,1)S(1)}, u32[]{:S(2)}, u32[]{:S(2)}) collective-permute-start(bf16[192,1792]{1,0:T(8,128)(2,1)S(1)} %convolution_convert_fusion.5), channel_id=1, source_target_pairs={{0,4},{4,8},{8,12},{12,16},{16,20},{20,24},{24,28},{28,0},{1,5},{5... | collective-permute-start | bytes 2064392 | tf_op jit(solution)/shard_map/ppermute | solution.py:23
  130.0 57.1 %collective-permute-start.9 = (bf16[192,1792]{1,0:T(8,128)(2,1)S(1)}, bf16[192,1792]{1,0:T(8,128)(2,1)S(1)}, u32[]{:S(2)}, u32[]{:S(2)}) collective-permute-start(bf16[192,1792]{1,0:T(8,128)(2,1)S(1)} %convolution_convert_fusion.4), channel_id=1, source_target_pairs={{0,28},{4,0},{8,4},{12,8},{16,12},{20,16},{24,20},{28,24},{1,29},{... | collective-permute-start | bytes 2064392 | tf_op jit(solution)/shard_map/ppermute | solution.py:23
Sparse Core Ops, SparseCore 0:
  124.3 38.4 reduce-scatter.1

commit v2 on v1

v2 whole, which is shorter than its diff:
```python
import functools
import math

import jax
import jax.numpy as jnp
from jax import lax
from jax.experimental import pallas as pl
from jax.experimental.pallas import tpu as pltpu
from jax.sharding import PartitionSpec as P

HD = 224
NEWCAP = 192
LANES = 128
GROUP = 4
WIDTH = GROUP * HD
FLOOR = -1e30
SCALE = 1.0 / math.sqrt(HD)
VMEM_LIMIT = 60 * 1024 * 1024
MESH = pl.DeviceIdType.MESH
WAYS = (1, -1)


def lane_iota(rows, columns):
    return lax.broadcasted_iota(jnp.int32, (rows, columns), 1)


def row_iota(rows, columns):
    return lax.broadcasted_iota(jnp.int32, (rows, columns), 0)


def attend_heads(query_of, key_of, value_of, live):
    tiles = [None] * (WIDTH // LANES)
    logs = []
    for head in range(GROUP):
        low, high = head * HD, (head + 1) * HD
        first, last = low // LANES, -(-high // LANES)
        a, b = first * LANES, last * LANES
        query = query_of(a, b)
        rows = query.shape[0]
        columns = lane_iota(rows, b - a)
        inside = (columns >= low - a) & (columns < high - a)
        part = jnp.where(inside, query, jnp.zeros((), query.dtype))
        scores = lax.dot_general(
            part, key_of(a, b), (((1,), (1,)), ((), ())), preferred_element_type=jnp.float32
        )
        scores = jnp.where(live, scores * SCALE, FLOOR)
        top = jnp.max(scores, axis=1, keepdims=True)
        weights = jnp.exp(scores - top)
        total = jnp.sum(weights, axis=1, keepdims=True)
        out = jnp.dot(
            weights.astype(jnp.bfloat16), value_of(a, b), preferred_element_type=jnp.float32
        ) / total
        logs.append(top + jnp.log(total))
        for tile in range(first, last):
            piece = out[:, tile * LANES - a : (tile + 1) * LANES - a]
            if tile * LANES < low:
                piece = jnp.where(
                    lane_iota(rows, LANES) >= low - tile * LANES, piece, tiles[tile]
                )
            tiles[tile] = piece
    return tiles, logs


def place(group, a, b):
    return pl.ds(pl.multiple_of(group * WIDTH + a, LANES), b - a)


def whole_kernel(
    count, chips, lens_ref, owner_ref, slot_ref, prior_ref,
    query_hbm, key_hbm, value_hbm, cache_key_hbm, cache_value_hbm, weight_hbm,
    mixed_ref, got_keys, got_values, tag_out,
    query, key, value, cache_key, cache_value, weight,
    query_out, key_out, value_out, query_in, tag_send, tag_in,
    result, answer, back, own, logs, held, part_a, part_b,
    near_a, near_b, far_send, far_in, local_sem, send_sem, recv_sem,
):
    rows, feat = query.shape
    cap = query_out.shape[1]
    prior = cache_key.shape[1]
    half = rows // 2
    span = rows // chips
    chunk = span // 2
    me, tp = lax.axis_index("req"), lax.axis_index("tp")
    chip, core = lax.div(tp, 2), lax.rem(tp, 2)
    sibling = chip * 2 + (1 - core)
    others = [lax.rem(chip + o, chips) for o in range(1, chips)]
    across = [other * 2 + core for other in others]
    beside = [lax.rem(me + 1, count), lax.rem(me + count - 1, count)]

    locals_ = [
        pltpu.make_async_copy(source, target, local_sem.at[i])
        for i, (source, target) in enumerate(
            (
                (query_hbm, query),
                (key_hbm, key),
                (value_hbm, value),
                (cache_key_hbm, cache_key),
                (cache_value_hbm, cache_value),
                (weight_hbm, weight),
            )
        )
    ]
    for copy in locals_:
        copy.start()

    barrier = pltpu.get_barrier_semaphore()
    partners = [{"req": beside[0]}, {"req": beside[1]}, {"tp": sibling}]
    partners += [{"tp": other} for other in across]
    for target in partners:
        pl.semaphore_signal(barrier, inc=1, device_id=target, device_id_type=MESH)
    pl.semaphore_wait(barrier, len(partners))

    def remote(number, source, target, device):
        return pltpu.make_async_remote_copy(
            src_ref=source,
            dst_ref=target,
            send_sem=send_sem.at[number],
            recv_sem=recv_sem.at[number],
            device_id=device,
            device_id_type=MESH,
        )

    def to_side(number, source, target, d, forth=True):
        device = {"req": beside[d] if forth else beside[1 - d]}
        return remote(number + d, source.at[d], target.at[d], device)

    starts = [jnp.int32(0)]
    for j in range(1, lens_ref.shape[1]):
        starts.append(starts[-1] + lens_ref[0, j - 1])
    next_is_first = owner_ref[0, 0] == beside[0]

    def by_way(a, b):
        return [jnp.where(next_is_first, a, b), jnp.where(next_is_first, b, a)]

    start = by_way(starts[0], starts[1])
    length = by_way(lens_ref[0, 0], lens_ref[0, 1])
    slot = by_way(slot_ref[0, 0], slot_ref[0, 1])
    limit = by_way(prior_ref[0, 0], prior_ref[0, 1])

    def pack(source, target, d):
        row, column = row_iota(cap, rows), lane_iota(cap, rows)
        hit = (column - start[d] == row) & (row < length[d])
        pick = jnp.where(hit, 1.0, 0.0).astype(jnp.bfloat16)

        def step(n, carry):
            at = pl.ds(pl.multiple_of(n * 256, 256), 256)
            target[d, :, at] = jnp.dot(
                pick, source[:, at], preferred_element_type=jnp.float32
            ).astype(jnp.bfloat16)
            return carry

        lax.fori_loop(0, feat // 256, step, 0)

    locals_[0].wait()
    tags, asks = [], []
    for d in range(2):
        tag_send[d] = jnp.where(row_iota(8, prior) == 0, slot[d], limit[d])
        pack(query, query_out, d)
        tags.append(to_side(0, tag_send, tag_in, d))
        asks.append(to_side(2, query_out, query_in, d))
        tags[d].start()
        asks[d].start()

    locals_[1].wait()
    locals_[2].wait()
    for d in range(2):
        pack(key, key_out, d)
        pack(value, value_out, d)

    logs[...] = jnp.zeros_like(logs)

    def own_group(group, carry):
        for begin in range(0, rows, half):
            end = begin + half
            row, column = begin + row_iota(half, end), lane_iota(half, end)
            first = jnp.zeros((half, end), jnp.int32)
            for s in starts[1:]:
                first = jnp.where(row >= s, s, first)
            tiles, sums = attend_heads(
                lambda a, b: query[begin:end, place(group, a, b)],
                lambda a, b: key[:end, place(group, a, b)],
                lambda a, b: value[:end, place(group, a, b)],
                (column >= first) & (column <= row),
            )
            for tile, piece in enumerate(tiles):
                at = place(group, tile * LANES, (tile + 1) * LANES)
                own[begin:end, at] = piece.astype(own.dtype)
            lanes = lane_iota(half, LANES)
            stat = logs[begin:end, :]
            for head in range(GROUP):
                stat = jnp.where(lanes == group * GROUP + head, sums[head], stat)
            logs[begin:end, :] = stat
        return carry

    lax.fori_loop(0, feat // WIDTH, own_group, 0)

    for d in range(2):
        tags[d].wait()
        asks[d].wait()
    key_sends = [to_side(4, key_out, got_keys, d) for d in range(2)]
    for copy in key_sends:
        copy.start()
    locals_[3].wait()
    locals_[4].wait()

    for i in range(2):
        result[i, :, feat:] = jnp.zeros((cap, LANES), result.dtype)

    groups = feat // WIDTH

    def prior_group(n, carry):
        i, group = n // groups, n % groups
        from_first = tag_in[0, 0:1, :] == i
        reach = jnp.where(from_first, tag_in[0, 1:2, :], tag_in[1, 1:2, :])

        def asked(a, b):
            at = place(group, a, b)
            first = jnp.broadcast_to(
                jnp.where(from_first[:, : b - a], 1.0, 0.0), (cap, b - a)
            )
            return jnp.where(
                first > 0.5,
                query_in[0, :, at].astype(jnp.float32),
                query_in[1, :, at].astype(jnp.float32),
            ).astype(jnp.bfloat16)

        tiles, sums = attend_heads(
            asked,
            lambda a, b: cache_key[i, :, place(group, a, b)],
            lambda a, b: cache_value[i, :, place(group, a, b)],
            lane_iota(cap, prior) < reach,
        )
        for tile, piece in enumerate(tiles):
            at = place(group, tile * LANES, (tile + 1) * LANES)
            result[i, :, at] = piece.astype(result.dtype)
        lanes = lane_iota(cap, LANES)
        stat = result[i, :, feat:].astype(jnp.float32)
        for head in range(GROUP):
            rest = sums[head]
            for part in range(3):
                rounded = rest.astype(jnp.bfloat16).astype(jnp.float32)
                stat = jnp.where(lanes == (group * GROUP + head) * 3 + part, rounded, stat)
                rest = rest - rounded
        result[i, :, feat:] = stat.astype(result.dtype)
        return carry

    lax.fori_loop(0, 2 * groups, prior_group, 0)

    def choose(n, carry):
        at = pl.ds(pl.multiple_of(n * LANES, LANES), LANES)
        first = jnp.broadcast_to(
            jnp.where(tag_in[0, 0:1, :LANES] == 0, 1.0, 0.0), (cap, LANES)
        )
        x, y = result[0, :, at].astype(jnp.float32), result[1, :, at].astype(jnp.float32)
        answer[0, :, at] = jnp.where(first > 0.5, x, y).astype(answer.dtype)
        answer[1, :, at] = jnp.where(first > 0.5, y, x).astype(answer.dtype)
        return carry

    lax.fori_loop(0, (feat + LANES) // LANES, choose, 0)
    tag_out[...] = tag_in[0, :, :LANES]
    backs = [to_side(6, answer, back, d, forth=False) for d in range(2)]
    for copy in backs:
        copy.start()
    for copy in backs:
        copy.wait()
    value_sends = [to_side(8, value_out, got_values, d) for d in range(2)]
    for copy in value_sends:
        copy.start()

    def merge(base):
        at_rows = pl.ds(pl.multiple_of(base, span), span)
        row, column = base + row_iota(span, cap), lane_iota(span, cap)
        spread = []
        for d in range(2):
            hit = (row - start[d] == column) & (column < length[d])
            spread.append(jnp.where(hit, 1.0, 0.0).astype(jnp.bfloat16))

        def placed(a, b):
            return jnp.dot(
                spread[0], back[0, :, a:b], preferred_element_type=jnp.float32
            ) + jnp.dot(spread[1], back[1, :, a:b], preferred_element_type=jnp.float32)

        stat = placed(feat, feat + LANES)
        mine = logs[at_rows, :]
        has = base + row_iota(span, 1) < starts[2]
        own_part, prior_part = [], []
        for head in range(feat // HD):
            far = stat[:, 3 * head : 3 * head + 1]
            far = far + stat[:, 3 * head + 1 : 3 * head + 2]
            far = far + stat[:, 3 * head + 2 : 3 * head + 3]
            near = mine[:, head : head + 1]
            top = jnp.maximum(near, far)
            x, y = jnp.exp(near - top), jnp.exp(far - top)
            own_part.append(jnp.where(has, x / (x + y), 1.0))
            prior_part.append(jnp.where(has, y / (x + y), 0.0))
        lanes = lane_iota(span, LANES)
        for pair in range(feat // 256):
            both = placed(pair * 256, pair * 256 + 256)
            for side in range(2):
                a = pair * 256 + side * LANES
                b = a + LANES
                h0, h1 = a // HD, (b - 1) // HD
                x, y = own_part[h0], prior_part[h0]
                if h1 != h0:
                    x = jnp.where(lanes < h1 * HD - a, x, own_part[h1])
                    y = jnp.where(lanes < h1 * HD - a, y, prior_part[h1])
                far = both[:, side * LANES : side * LANES + LANES]
                total = own[at_rows, a:b].astype(jnp.float32) * x + far * y
                held[:, a:b] = total.astype(jnp.bfloat16)

    def project(target):
        def step(n, carry):
            at = pl.ds(pl.multiple_of(n * 512, 512), 512)
            target[:, at] = jnp.dot(
                held[...], weight[:, at], preferred_element_type=jnp.float32
            ).astype(target.dtype)
            return carry

        lax.fori_loop(0, weight.shape[1] // 512, step, 0)

    def chunk_of(n):
        return pl.ds(pl.multiple_of(n * chunk, chunk), chunk)

    locals_[5].wait()
    overs = []
    for n in range(chips - 1):
        merge(others[n] * span)
        project(part_a.at[n])
        near = remote(
            11 + n, part_a.at[n, chunk_of(1 - core), :], near_a.at[n], {"tp": sibling}
        )
        near.start()
        near.wait()
        far_send[n] = (
            part_a[n, chunk_of(core), :].astype(jnp.float32) + near_a[n].astype(jnp.float32)
        ).astype(far_send.dtype)
        overs.append(
            remote(10 + chips + n, far_send.at[n], far_in.at[n], {"tp": across[n]})
        )
        overs[n].start()
    merge(chip * span)
    project(part_b)
    last = remote(10, part_b.at[chunk_of(1 - core), :], near_b, {"tp": sibling})
    last.start()
    last.wait()
    total = part_b[chunk_of(core), :].astype(jnp.float32) + near_b[...].astype(jnp.float32)
    for n in range(chips - 1):
        overs[n].wait()
        total = total + far_in[n].astype(jnp.float32)
    mixed_ref[...] = total.astype(mixed_ref.dtype)
    for copy in key_sends + value_sends:
        copy.wait()


def body(
    queries,
    keys_new,
    values_new,
    cache_keys,
    cache_values,
    out_proj,
    req_lengths,
    cache_owner,
    cache_slot,
    prior_len,
):
    rows, feat = queries.shape
    width = out_proj.shape[1]
    slots, prior = cache_keys.shape[:2]
    chips = lax.axis_size("tp") // 2
    span = rows // chips
    chunk = span // 2
    bf16 = jnp.bfloat16
    packed = (2, NEWCAP, feat)
    answers = (2, NEWCAP, feat + LANES)
    smem = pl.BlockSpec(memory_space=pltpu.SMEM)
    hbm = pl.BlockSpec(memory_space=pl.ANY)
    vmem = pl.BlockSpec(memory_space=pltpu.VMEM)
    mixed, got_keys, got_values, tag = pl.pallas_call(
        functools.partial(whole_kernel, lax.axis_size("req"), chips),
        in_specs=[smem] * 4 + [hbm] * 6,
        out_specs=[vmem, hbm, hbm, vmem],
        out_shape=[
            jax.ShapeDtypeStruct((chunk, width), bf16),
            jax.ShapeDtypeStruct(packed, bf16),
            jax.ShapeDtypeStruct(packed, bf16),
            jax.ShapeDtypeStruct((8, LANES), jnp.int32),
        ],
        scratch_shapes=[
            pltpu.VMEM((rows, feat), bf16),
            pltpu.VMEM((rows, feat), bf16),
            pltpu.VMEM((rows, feat), bf16),
            pltpu.VMEM(cache_keys.shape, bf16),
            pltpu.VMEM(cache_values.shape, bf16),
            pltpu.VMEM(out_proj.shape, bf16),
            pltpu.VMEM(packed, bf16),
            pltpu.VMEM(packed, bf16),
            pltpu.VMEM(packed, bf16),
            pltpu.VMEM(packed, bf16),
            pltpu.VMEM((2, 8, prior), jnp.int32),
            pltpu.VMEM((2, 8, prior), jnp.int32),
            pltpu.VMEM(answers, bf16),
            pltpu.VMEM(answers, bf16),
            pltpu.VMEM(answers, bf16),
            pltpu.VMEM((rows, feat), bf16),
            pltpu.VMEM((rows, LANES), jnp.float32),
            pltpu.VMEM((span, feat), bf16),
            pltpu.VMEM((chips - 1, span, width), bf16),
            pltpu.VMEM((span, width), bf16),
            pltpu.VMEM((chips - 1, chunk, width), bf16),
            pltpu.VMEM((chunk, width), bf16),
            pltpu.VMEM((chips - 1, chunk, width), bf16),
            pltpu.VMEM((chips - 1, chunk, width), bf16),
            pltpu.SemaphoreType.DMA((6,)),
            pltpu.SemaphoreType.DMA((9 + 2 * chips,)),
            pltpu.SemaphoreType.DMA((9 + 2 * chips,)),
        ],
        compiler_params=pltpu.CompilerParams(
            collective_id=0, has_side_effects=True, vmem_limit_bytes=VMEM_LIMIT
        ),
        cost_estimate=pl.CostEstimate(
            flops=2 * rows * feat * width, bytes_accessed=37_000_000, transcendentals=5_000_000
        ),
        name="whole",
    )(
        req_lengths, cache_owner, cache_slot, prior_len,
        queries, keys_new, values_new, cache_keys, cache_values, out_proj,
    )
    slot_ids = jnp.arange(slots, dtype=jnp.int32)[:, None, None]
    first = slot_ids == tag[0, 0]
    new_keys = jnp.where(first, got_keys[0][None], got_keys[1][None])
    new_values = jnp.where(first, got_values[0][None], got_values[1][None])
    return (mixed, new_keys, new_values)


def solution(mesh):
    in_specs = (
        P("req", "tp"),
        P("req", "tp"),
        P("req", "tp"),
        P("req", None, "tp"),
        P("req", None, "tp"),
        P("tp", None),
        P("req", None),
        P("req", None),
        P("req", None),
        P("req", None),
    )
    out_specs = (P(("req", "tp"), None), P("req", None, "tp"), P("req", None, "tp"))
    return jax.shard_map(body, mesh=mesh, in_specs=in_specs, out_specs=out_specs, check_vma=False)
```

time: 196 us -> 144 us (0.73)
  Pallas kernels: 40.7 us -> 136 us
  waiting for transfers between devices: 86.1 us -> 0 us
  between operations: 25.7 us -> 0.66 us
  starting transfers between devices: 25 us -> 0 us
  matrix products: 9.83 us -> 0 us
    pallas_call x4 -> x1, Pallas kernels: 40.7 us -> 136 us  [body(): pl.pallas_call(functools.partial(whole_kernel, lax.axis_size('req'), chip...]
    ppermute x10 -> x0, waiting for transfers between devices: 86.1 us -> none  [shifted(): return lax.ppermute(value, axis, pairs)]
    ppermute x10 -> x0, starting transfers between devices: 25 us -> none  [shifted(): return lax.ppermute(value, axis, pairs)]
    dot_general x6 -> x0, matrix products: 9.83 us -> none  [pick_rows(): jnp.dot(hit.astype(jnp.bfloat16), source, preferred_element_type=jnp.floa...]
    slice x3 -> x1, local copies, waits for them, and re-layouts: 4.13 us -> 1.18 us  [body(): first = slot_ids == tag[0, 0]]
  transfers between devices with their start and end apart: 11 -> 0, of which waited for: 8 -> 0; matrix products, arithmetic and copies ran while one was open for 7% -> 0% of each run, Pallas kernels for 12% -> 0%
where the time goes in v2:
time: 144 us; the launch traced here: 143 us
  Pallas kernels  136 us (94%)
  local copies, waits for them, and re-layouts  4.01 us (3%)
  other arithmetic  2.5 us (2%)
    pallas_call x1, Pallas kernels, body(): pl.pallas_call(functools.partial(whole_kernel, lax.axis_size('req'), chip...  136 us

profile of v2, /device:TPU:0, one launch (start us, length us, event | category | flops | bytes accessed | tf_op | source)
XLA Modules:
  0.0 143.5 jit_solution(2189712821244540892)
XLA Ops:
  0.6 136.3 %whole.1 = (bf16[128,3584]{1,0:T(8,128)(2,1)}, bf16[2,192,1792]{2,1,0:T(8,128)(2,1)}, bf16[2,192,1792]{2,1,0:T(8,128)(2,1)}, s32[8,128]{1,0:T(8,128)}) custom-call(s32[1,4]{1,0:T(1,128)} %lens_ref.1, s32[1,2]{1,0:T(1,128)} %owner_ref.1, s32[1,2]{1,0:T(1,128)} %slot_ref.1, s32[1,2]{1,0:T(1,128)} %prior_ref.1, bf16[512,1792]{1,0:T(8,128)(2,1)} %query_hbm.1, ...), custom_call_target="tpu_custom_call" | custom-call | flops 6576668672 | bytes 37000000 | tf_op jit(solution)/shard_map/whole/pallas_call | solution.py:379
  136.9 1.2 slice.15
  138.1 0.6 iota_compare_fusion
  138.8 1.9 %slice_bitcast_fusion.1 = (bf16[192,1792]{1,0:T(8,128)(2,1)S(1)}, bf16[192,1792]{1,0:T(8,128)(2,1)S(1)}, bf16[192,1792]{1,0:T(8,128)(2,1)S(1)}, bf16[192,1792]{1,0:T(8,128)(2,1)S(1)}) fusion(bf16[2,192,1792]{2,1,0:T(8,128)(2,1)} %get-tuple-element.10, bf16[2,192,1792]{2,1,0:T(8,128)(2,1)} %get-tuple-element.9), kind=kLoop, calls=%fused_computation.3 | loop fusion | bytes 5505024 | tf_op jit(solution)/shard_map/jit(_where)/broadcast_in_dim | solution.py:432
  140.7 0.0 copy-start
  140.7 1.9 %broadcast_select_fusion = (bf16[2,192,1792]{2,1,0:T(8,128)(2,1)}, bf16[2,192,1792]{2,1,0:T(8,128)(2,1)}) fusion(pred[2]{0:T(512)(128)(4,1)S(1)} %iota_compare_fusion, bf16[192,1792]{1,0:T(8,128)(2,1)S(1)} %get-tuple-element.12, bf16[192,1792]{1,0:T(8,128)(2,1)S(1)} %get-tuple-element.11, bf16[192,1792]{1,0:T(8,128)(2,1)S(1)} %get-tuple-element.17, ...), kind=kLoop, calls=%fused_computation | loop fusion | flops 1376256 | bytes 5505026 | tf_op jit(solution)/shard_map/jit(_where)/select_n | solution.py:432
  142.6 0.0 copy-done
  142.6 0.9 copy.14
Async XLA Ops:
  140.7 1.9 %copy-start = (bf16[128,3584]{1,0:T(8,128)(2,1)S(1)}, bf16[128,3584]{1,0:T(8,128)(2,1)}, u32[]{:S(2)}) copy-start(bf16[128,3584]{1,0:T(8,128)(2,1)} %get-tuple-element.22) | copy-start | bytes 2752516

commit v3 on v2

--- a/solution.py
+++ b/solution.py
@@ -68,10 +68,10 @@
 def whole_kernel(
     count, chips, lens_ref, owner_ref, slot_ref, prior_ref,
     query_hbm, key_hbm, value_hbm, cache_key_hbm, cache_value_hbm, weight_hbm,
-    mixed_ref, got_keys, got_values, tag_out,
+    mixed_ref, got_key_first, got_key_second, got_value_first, got_value_second, tag_out,
     query, key, value, cache_key, cache_value, weight,
     query_out, key_out, value_out, query_in, tag_send, tag_in,
-    result, answer, back, own, logs, held, part_a, part_b,
+    result, sums_out, answer, back, sums_answer, sums_back, own, logs, held, part_a, part_b,
     near_a, near_b, far_send, far_in, local_sem, send_sem, recv_sem,
 ):
     rows, feat = query.shape
@@ -100,8 +100,7 @@
             )
         )
     ]
-    for copy in locals_:
-        copy.start()
+    locals_[0].start()
 
     barrier = pltpu.get_barrier_semaphore()
     partners = [{"req": beside[0]}, {"req": beside[1]}, {"tp": sibling}]
@@ -124,6 +123,12 @@
         device = {"req": beside[d] if forth else beside[1 - d]}
         return remote(number + d, source.at[d], target.at[d], device)
 
+    got_keys = (got_key_first, got_key_second)
+    got_values = (got_value_first, got_value_second)
+
+    def store_to(number, source, target, d, at):
+        return remote(number + d, source.at[d, at, :], target[d].at[at, :], {"req": beside[d]})
+
     starts = [jnp.int32(0)]
     for j in range(1, lens_ref.shape[1]):
         starts.append(starts[-1] + lens_ref[0, j - 1])
@@ -152,6 +157,8 @@
         lax.fori_loop(0, feat // 256, step, 0)
 
     locals_[0].wait()
+    for copy in locals_[1:]:
+        copy.start()
     tags, asks = [], []
     for d in range(2):
         tag_send[d] = jnp.where(row_iota(8, prior) == 0, slot[d], limit[d])
@@ -194,17 +201,21 @@
 
     lax.fori_loop(0, feat // WIDTH, own_group, 0)
 
+    early, late = pl.ds(0, cap // 2), pl.ds(cap // 2, cap // 2)
     for d in range(2):
-        tags[d].wait()
-        asks[d].wait()
-    key_sends = [to_side(4, key_out, got_keys, d) for d in range(2)]
-    for copy in key_sends:
+        tags[d].wait_send()
+        asks[d].wait_send()
+    stores = [store_to(4, key_out, got_keys, d, early) for d in range(2)]
+    for copy in stores:
         copy.start()
+    for d in range(2):
+        tags[d].wait_recv()
+        asks[d].wait_recv()
     locals_[3].wait()
     locals_[4].wait()
 
     for i in range(2):
-        result[i, :, feat:] = jnp.zeros((cap, LANES), result.dtype)
+        sums_out[i] = jnp.zeros((cap, LANES), sums_out.dtype)
 
     groups = feat // WIDTH
 
@@ -234,14 +245,14 @@
             at = place(group, tile * LANES, (tile + 1) * LANES)
             result[i, :, at] = piece.astype(result.dtype)
         lanes = lane_iota(cap, LANES)
-        stat = result[i, :, feat:].astype(jnp.float32)
+        stat = sums_out[i].astype(jnp.float32)
         for head in range(GROUP):
             rest = sums[head]
             for part in range(3):
                 rounded = rest.astype(jnp.bfloat16).astype(jnp.float32)
                 stat = jnp.where(lanes == (group * GROUP + head) * 3 + part, rounded, stat)
                 rest = rest - rounded
-        result[i, :, feat:] = stat.astype(result.dtype)
+        sums_out[i] = stat.astype(sums_out.dtype)
         return carry
 
     lax.fori_loop(0, 2 * groups, prior_group, 0)
@@ -256,16 +267,35 @@
         answer[1, :, at] = jnp.where(first > 0.5, y, x).astype(answer.dtype)
         return carry
 
-    lax.fori_loop(0, (feat + LANES) // LANES, choose, 0)
+    lax.fori_loop(0, feat // LANES, choose, 0)
+    first = jnp.broadcast_to(jnp.where(tag_in[0, 0:1, :LANES] == 0, 1.0, 0.0), (cap, LANES))
+    x, y = sums_out[0].astype(jnp.float32), sums_out[1].astype(jnp.float32)
+    held_rows = sums_answer.shape[1]
+    unit = jnp.where(
+        row_iota(held_rows, LANES) == lane_iota(held_rows, LANES), 1.0, 0.0
+    ).astype(jnp.bfloat16)
+    for d, chosen in enumerate((jnp.where(first > 0.5, x, y), jnp.where(first > 0.5, y, x))):
+        sums_answer[d] = lax.dot_general(
+            unit,
+            chosen.astype(jnp.bfloat16),
+            (((1,), (1,)), ((), ())),
+            preferred_element_type=jnp.float32,
+        ).astype(jnp.bfloat16)
     tag_out[...] = tag_in[0, :, :LANES]
-    backs = [to_side(6, answer, back, d, forth=False) for d in range(2)]
+    backs = [to_side(12, sums_answer, sums_back, d, forth=False) for d in range(2)]
+    backs += [to_side(10, answer, back, d, forth=False) for d in range(2)]
     for copy in backs:
         copy.start()
     for copy in backs:
-        copy.wait()
-    value_sends = [to_side(8, value_out, got_values, d) for d in range(2)]
-    for copy in value_sends:
+        copy.wait_send()
+    for copy in (
+        [store_to(6, key_out, got_keys, d, late) for d in range(2)]
+        + [store_to(8, value_out, got_values, d, pl.ds(0, cap)) for d in range(2)]
+    ):
         copy.start()
+        stores.append(copy)
+    for copy in backs:
+        copy.wait_recv()
 
     def merge(base):
         at_rows = pl.ds(pl.multiple_of(base, span), span)
@@ -280,7 +310,15 @@
                 spread[0], back[0, :, a:b], preferred_element_type=jnp.float32
             ) + jnp.dot(spread[1], back[1, :, a:b], preferred_element_type=jnp.float32)
 
-        stat = placed(feat, feat + LANES)
+        stat = sum(
+            lax.dot_general(
+                spread[d],
+                sums_back[d],
+                (((1,), (1,)), ((), ())),
+                preferred_element_type=jnp.float32,
+            )
+            for d in range(2)
+        )
         mine = logs[at_rows, :]
         has = base + row_iota(span, 1) < starts[2]
         own_part, prior_part = [], []
@@ -327,7 +365,7 @@
         merge(others[n] * span)
         project(part_a.at[n])
         near = remote(
-            11 + n, part_a.at[n, chunk_of(1 - core), :], near_a.at[n], {"tp": sibling}
+            15 + n, part_a.at[n, chunk_of(1 - core), :], near_a.at[n], {"tp": sibling}
         )
         near.start()
         near.wait()
@@ -335,12 +373,12 @@
             part_a[n, chunk_of(core), :].astype(jnp.float32) + near_a[n].astype(jnp.float32)
         ).astype(far_send.dtype)
         overs.append(
-            remote(10 + chips + n, far_send.at[n], far_in.at[n], {"tp": across[n]})
+            remote(14 + chips + n, far_send.at[n], far_in.at[n], {"tp": across[n]})
         )
         overs[n].start()
     merge(chip * span)
     project(part_b)
-    last = remote(10, part_b.at[chunk_of(1 - core), :], near_b, {"tp": sibling})
+    last = remote(14, part_b.at[chunk_of(1 - core), :], near_b, {"tp": sibling})
     last.start()
     last.wait()
     total = part_b[chunk_of(core), :].astype(jnp.float32) + near_b[...].astype(jnp.float32)
@@ -348,7 +386,7 @@
         overs[n].wait()
         total = total + far_in[n].astype(jnp.float32)
     mixed_ref[...] = total.astype(mixed_ref.dtype)
-    for copy in key_sends + value_sends:
+    for copy in stores:
         copy.wait()
 
 
@@ -372,18 +410,20 @@
     chunk = span // 2
     bf16 = jnp.bfloat16
     packed = (2, NEWCAP, feat)
-    answers = (2, NEWCAP, feat + LANES)
+    sums = (2, -(-3 * (feat // HD) // 16) * 16, NEWCAP)
     smem = pl.BlockSpec(memory_space=pltpu.SMEM)
     hbm = pl.BlockSpec(memory_space=pl.ANY)
     vmem = pl.BlockSpec(memory_space=pltpu.VMEM)
-    mixed, got_keys, got_values, tag = pl.pallas_call(
+    mixed, key_first, key_second, value_first, value_second, tag = pl.pallas_call(
         functools.partial(whole_kernel, lax.axis_size("req"), chips),
         in_specs=[smem] * 4 + [hbm] * 6,
-        out_specs=[vmem, hbm, hbm, vmem],
+        out_specs=[vmem, hbm, hbm, hbm, hbm, vmem],
         out_shape=[
             jax.ShapeDtypeStruct((chunk, width), bf16),
-            jax.ShapeDtypeStruct(packed, bf16),
-            jax.ShapeDtypeStruct(packed, bf16),
+            jax.ShapeDtypeStruct(packed[1:], bf16),
+            jax.ShapeDtypeStruct(packed[1:], bf16),
+            jax.ShapeDtypeStruct(packed[1:], bf16),
+            jax.ShapeDtypeStruct(packed[1:], bf16),
             jax.ShapeDtypeStruct((8, LANES), jnp.int32),
         ],
         scratch_shapes=[
@@ -399,9 +439,12 @@
             pltpu.VMEM(packed, bf16),
             pltpu.VMEM((2, 8, prior), jnp.int32),
             pltpu.VMEM((2, 8, prior), jnp.int32),
-            pltpu.VMEM(answers, bf16),
-            pltpu.VMEM(answers, bf16),
-            pltpu.VMEM(answers, bf16),
+            pltpu.VMEM(packed, bf16),
+            pltpu.VMEM((2, NEWCAP, LANES), bf16),
+            pltpu.VMEM(packed, bf16),
+            pltpu.VMEM(packed, bf16),
+            pltpu.VMEM(sums, bf16),
+            pltpu.VMEM(sums, bf16),
             pltpu.VMEM((rows, feat), bf16),
             pltpu.VMEM((rows, LANES), jnp.float32),
             pltpu.VMEM((span, feat), bf16),
@@ -412,8 +455,8 @@
             pltpu.VMEM((chips - 1, chunk, width), bf16),
             pltpu.VMEM((chips - 1, chunk, width), bf16),
             pltpu.SemaphoreType.DMA((6,)),
-            pltpu.SemaphoreType.DMA((9 + 2 * chips,)),
-            pltpu.SemaphoreType.DMA((9 + 2 * chips,)),
+            pltpu.SemaphoreType.DMA((13 + 2 * chips,)),
+            pltpu.SemaphoreType.DMA((13 + 2 * chips,)),
         ],
         compiler_params=pltpu.CompilerParams(
             collective_id=0, has_side_effects=True, vmem_limit_bytes=VMEM_LIMIT
@@ -428,8 +471,8 @@
     )
     slot_ids = jnp.arange(slots, dtype=jnp.int32)[:, None, None]
     first = slot_ids == tag[0, 0]
-    new_keys = jnp.where(first, got_keys[0][None], got_keys[1][None])
-    new_values = jnp.where(first, got_values[0][None], got_values[1][None])
+    new_keys = jnp.where(first, key_first[None], key_second[None])
+    new_values = jnp.where(first, value_first[None], value_second[None])
     return (mixed, new_keys, new_values)
 
 

time: 144 us -> 147 us (1.021)
  Pallas kernels: 136 us -> 140 us
  local copies, waits for them, and re-layouts: 4.01 us -> 2.12 us
  other arithmetic: 2.5 us -> 4.3 us
    pallas_call x1, Pallas kernels: 136 us -> 140 us  [body(): pl.pallas_call(functools.partial(whole_kernel, lax.axis_size('req'), chip...]
    broadcast_in_dim x1 -> x0, local copies, waits for them, and re-layouts: 1.9 us -> none  [body(): new_values = jnp.where(first, got_values[0][None], got_values[1][None])]
    select_n x1, other arithmetic: 1.85 us -> 3.66 us  [body(): new_values = jnp.where(first, value_first[None], value_second[None])]
where the time goes in v3:
time: 147 us
  Pallas kernels  140 us (95%)
  other arithmetic  4.3 us (3%)
  local copies, waits for them, and re-layouts  2.12 us (1%)
    pallas_call x1, Pallas kernels, body(): pl.pallas_call(functools.partial(whole_kernel, lax.axis_size('req'), chip...  140 us
    select_n x1, other arithmetic, body(): new_values = jnp.where(first, value_first[None], value_second[None])  3.66 us

profile of v3, /device:TPU:0, one launch (start us, length us, event | category | flops | bytes accessed | tf_op | source)
XLA Modules:
  0.0 146.9 jit_solution(15558991064395806189)
XLA Ops:
  0.6 139.8 %whole.1 = (bf16[128,3584]{1,0:T(8,128)(2,1)}, bf16[192,1792]{1,0:T(8,128)(2,1)}, bf16[192,1792]{1,0:T(8,128)(2,1)}, bf16[192,1792]{1,0:T(8,128)(2,1)}, bf16[192,1792]{1,0:T(8,128)(2,1)}, /*index=5*/s32[8,128]{1,0:T(8,128)}) custom-call(s32[1,4]{1,0:T(1,128)} %lens_ref.1, s32[1,2]{1,0:T(1,128)} %owner_ref.1, s32[1,2]{1,0:T(1,128)} %slot_ref.1, ...), custom_call_target="tpu_custom_call" | custom-call | flops 6576668672 | bytes 37000000 | tf_op jit(solution)/shard_map/whole/pallas_call | solution.py:417
  140.4 1.2 slice.3
  141.6 0.6 iota_compare_fusion
  142.3 0.0 copy-start
  142.3 3.7 %broadcast_select_fusion = (bf16[2,192,1792]{2,1,0:T(8,128)(2,1)}, bf16[2,192,1792]{2,1,0:T(8,128)(2,1)}) fusion(pred[2]{0:T(512)(128)(4,1)S(1)} %iota_compare_fusion, bf16[192,1792]{1,0:T(8,128)(2,1)} %get-tuple-element.14, bf16[192,1792]{1,0:T(8,128)(2,1)} %get-tuple-element.13, bf16[192,1792]{1,0:T(8,128)(2,1)} %get-tuple-element.12, ...), kind=kLoop, calls=%fused_computation | loop fusion | flops 1376256 | bytes 5505026 | tf_op jit(solution)/shard_map/jit(_where)/select_n | solution.py:475
  145.9 0.0 copy-done
  145.9 0.9 copy.14
Async XLA Ops:
  142.3 3.7 %copy-start = (bf16[128,3584]{1,0:T(8,128)(2,1)S(1)}, bf16[128,3584]{1,0:T(8,128)(2,1)}, u32[]{:S(2)}) copy-start(bf16[128,3584]{1,0:T(8,128)(2,1)} %get-tuple-element.20) | copy-start | bytes 2752516
